TPU v7x, 512 devices: a whole 4x8x8 slice. The times are simulated.
512 devices in a mesh: ctx: 64 (over z, y_hi, x), ch: 8 (over y_lo, core).
Axes of the slice: x: 4, y: 8 (y_hi: 2, y_lo: 4; y = y_hi * 4 + y_lo), z: 8, core: 2. Of those that a mesh axis runs over, the one named last changes fastest.
Arguments:
- post_gate: bfloat16 [2, 4096, 8192], P(None, 'ctx', 'ch'), may hold values from -6 to 6
- pre_gate: bfloat16 [2, 4096, 8192], P(None, 'ctx', 'ch'), may hold values from -6 to 6
- signal: bfloat16 [2, 4096, 8192], P(None, 'ctx', 'ch'), may hold values from -6 to 6
- long_filter: bfloat16 [4096, 8192], P('ctx', 'ch'), may hold values from -1 to 1
- out_weight: bfloat16 [8192, 4096], P('ch', 'ctx'), may hold values from -0.0625 to 0.0625
Outputs:
- layer_out: bfloat16 [2, 4096, 4096], P(None, 'ctx', 'ch')
All inputs are finite; a program needn't handle non-finite values.
Results may differ from a plain program's by a relative error of at most 0.025.
Values may be sent and summed in bfloat16 or wider, within the bound.
A program may use at most 64 MiB of HBM per device.

v0:
```python
import math

import jax
import jax.numpy as jnp
from jax import lax
from jax.sharding import PartitionSpec as P


def angle_table(left, right, modulus):
    product = left[:, None] * right[None, :] % modulus
    return product.astype(jnp.float32) * (2.0 * math.pi / modulus)


def split_table(table):
    table_high = table.astype(jnp.bfloat16)
    table_low = (table - table_high.astype(jnp.float32)).astype(jnp.bfloat16)
    return (table_high, table_low)


def across_blocks(table, values):
    table_high, table_low = split_table(table)
    upper_part = jnp.einsum("qn,bnmc->bqmc", table_high, values, preferred_element_type=jnp.float32)
    lower_part = jnp.einsum("qn,bnmc->bqmc", table_low, values, preferred_element_type=jnp.float32)
    return upper_part + lower_part


def within_block(table, values):
    table_high, table_low = split_table(table)
    upper_part = jnp.einsum("qn,bknc->bkqc", table_high, values, preferred_element_type=jnp.float32)
    lower_part = jnp.einsum("qn,bknc->bkqc", table_low, values, preferred_element_type=jnp.float32)
    return upper_part + lower_part


def within_float(table, values):
    return jnp.einsum("qn,bknc->bkqc", table, values, precision=lax.Precision.HIGHEST)


def first_section(blocks, first_offset, span):
    count = blocks.shape[1]
    width = blocks.shape[2]
    freq = jnp.arange(2 * count, dtype=jnp.int32)
    theta = angle_table(freq, jnp.arange(count, dtype=jnp.int32), 2 * count)
    real_part = across_blocks(jnp.cos(theta), blocks)
    imag_part = -across_blocks(jnp.sin(theta), blocks)
    offsets = first_offset + jnp.arange(width, dtype=jnp.int32)
    phase = angle_table(freq, offsets, span)
    cos_tw = jnp.cos(phase)[None, :, :, None]
    sin_tw = jnp.sin(phase)[None, :, :, None]
    out_real = (real_part * cos_tw + imag_part * sin_tw).astype(jnp.bfloat16)
    out_imag = (imag_part * cos_tw - real_part * sin_tw).astype(jnp.bfloat16)
    return jnp.stack([out_real, out_imag], axis=1)


def spectral_product(spectra, first_freq, span):
    real_in, imag_in = (spectra[:, 0], spectra[:, 1])
    width = real_in.shape[2]
    inner = jnp.arange(width, dtype=jnp.int32)
    theta = angle_table(inner, inner, width)
    cos_tab, sin_tab = (jnp.cos(theta), jnp.sin(theta))
    spec_real = within_block(cos_tab, real_in) + within_block(sin_tab, imag_in)
    spec_imag = within_block(cos_tab, imag_in) - within_block(sin_tab, real_in)
    filt_real, filt_imag = (spec_real[0:1], spec_imag[0:1])
    sig_real, sig_imag = (spec_real[1:], spec_imag[1:])
    prod_real = filt_real * sig_real - filt_imag * sig_imag
    prod_imag = filt_real * sig_imag + filt_imag * sig_real
    mid_real = within_float(cos_tab, prod_real) - within_float(sin_tab, prod_imag)
    mid_imag = within_float(cos_tab, prod_imag) + within_float(sin_tab, prod_real)
    freq = first_freq + jnp.arange(real_in.shape[1], dtype=jnp.int32)
    phase = angle_table(freq, inner, span)
    cos_tw = jnp.cos(phase)[None, :, :, None]
    sin_tw = jnp.sin(phase)[None, :, :, None]
    back_real = (mid_real * cos_tw - mid_imag * sin_tw).astype(jnp.bfloat16)
    back_imag = (mid_imag * cos_tw + mid_real * sin_tw).astype(jnp.bfloat16)
    return jnp.stack([back_real, back_imag], axis=1)


def last_section(back_pair, span):
    count = back_pair.shape[2] // 2
    theta = angle_table(
        jnp.arange(count, dtype=jnp.int32), jnp.arange(2 * count, dtype=jnp.int32), 2 * count
    )
    summed = across_blocks(jnp.cos(theta), back_pair[:, 0]) - across_blocks(
        jnp.sin(theta), back_pair[:, 1]
    )
    return (summed / span).astype(jnp.bfloat16)


def on_device(post_gate, pre_gate, signal, long_filter, out_weight):
    seqs, width, channels = signal.shape
    blocks = lax.axis_size("ctx")
    span = 2 * blocks * width
    inner = (pre_gate.astype(jnp.float32) * signal.astype(jnp.float32)).astype(jnp.bfloat16)
    stacked = jnp.concatenate([long_filter[None], inner], axis=0)
    stacked = stacked.reshape(seqs + 1, 1, width, channels)
    per_dev = width // blocks
    position = lax.axis_index("ctx")
    spread = lax.all_to_all(stacked, "ctx", split_axis=2, concat_axis=1, tiled=True)
    first = first_section(spread, position * per_dev, span)
    spectra = lax.all_to_all(first, "ctx", split_axis=2, concat_axis=3, tiled=True)
    back_pair = spectral_product(spectra, position * 2, span)
    back_blocks = lax.all_to_all(back_pair, "ctx", split_axis=3, concat_axis=2, tiled=True)
    convolved = last_section(back_blocks, span)
    returned = lax.all_to_all(convolved, "ctx", split_axis=1, concat_axis=2, tiled=True)
    returned = returned.reshape(seqs, width, channels)
    gated = (post_gate.astype(jnp.float32) * returned.astype(jnp.float32)).astype(jnp.bfloat16)
    partial_value = jnp.einsum(
        "sjc,co->sjo",
        gated,
        lax.all_gather(out_weight, "ctx", axis=1, tiled=True),
        preferred_element_type=jnp.float32,
    )
    summed = lax.psum_scatter(
        partial_value.astype(jnp.bfloat16), "ch", scatter_dimension=2, tiled=True
    )
    return summed


def solution(mesh):
    return jax.shard_map(
        on_device,
        mesh=mesh,
        in_specs=(
            P(None, "ctx", "ch"),
            P(None, "ctx", "ch"),
            P(None, "ctx", "ch"),
            P("ctx", "ch"),
            P("ch", "ctx"),
        ),
        out_specs=P(None, "ctx", "ch"),
        check_vma=False,
    )
```

profile of v0, /device:TPU:4, one launch (start us, length us, event | category | flops | bytes accessed | tf_op | source)
XLA Modules:
  0.0 297.1 jit_solution(12324933738468128904)
XLA Ops:
  6.5 0.7 all-gather.2.cloned.1.call-update
  7.3 1.1 multiply_convert_fusion
  8.4 0.9 maximum_bitcast_fusion
  9.3 1.2 copy.53
  10.5 19.1 %all-to-all-start = ((bf16[3,1,64,1024]{3,0,1,2:T(4,128)(2,1)}), bf16[3,1,64,1024]{3,0,1,2:T(4,128)(2,1)S(1)}, u32[]{:S(2)}, u32[]{:S(2)}) async-start(bf16[3,1,64,1024]{3,0,1,2:T(4,128)(2,1)} %copy.53), calls=%async_computation | async-start | bytes 1048576 | tf_op jit(solution)/shard_map/all_to_all | solution.py:97
  29.6 18.6 %all-to-all-done = bf16[3,1,64,1024]{3,0,1,2:T(4,128)(2,1)S(1)} async-done(((bf16[3,1,64,1024]{3,0,1,2:T(4,128)(2,1)}), bf16[3,1,64,1024]{3,0,1,2:T(4,128)(2,1)S(1)}, u32[]{:S(2)}, u32[]{:S(2)}) %all-to-all-start) | async-done | bytes 393248 | tf_op jit(solution)/shard_map/all_to_all | solution.py:97
  48.3 0.5 fusion.25
  48.8 0.5 fusion.28
  49.4 0.6 add_negate_fusion
  49.9 0.9 fusion.14
  50.9 3.1 %copy.55 = bf16[3,2,128,1,1024]{4,1,3,0,2:T(2,128)(2,1)} copy(bf16[3,2,128,1,1024]{2,4,0,3,1:T(8,128)(2,1)S(1)} %pad_maximum_fusion) | data formatting | bytes 3145728 | tf_op jit(solution)/shard_map/stack | solution.py:51
  54.0 9.8 %all-to-all-start.1 = ((bf16[3,2,128,1,1024]{4,1,3,0,2:T(2,128)(2,1)}), bf16[3,2,128,1,1024]{4,1,3,0,2:T(2,128)(2,1)S(1)}, u32[]{:S(2)}, u32[]{:S(2)}) async-start(bf16[3,2,128,1,1024]{4,1,3,0,2:T(2,128)(2,1)} %copy.55), calls=%async_computation.1 | async-start | bytes 3145728 | tf_op jit(solution)/shard_map/all_to_all | solution.py:99
  64.2 39.5 %all-to-all-done.1 = bf16[3,2,128,1,1024]{4,1,3,0,2:T(2,128)(2,1)S(1)} async-done(((bf16[3,2,128,1,1024]{4,1,3,0,2:T(2,128)(2,1)}), bf16[3,2,128,1,1024]{4,1,3,0,2:T(2,128)(2,1)S(1)}, u32[]{:S(2)}, u32[]{:S(2)}) %all-to-all-start.1) | async-done | bytes 1572896 | tf_op jit(solution)/shard_map/all_to_all | solution.py:99
  103.7 0.5 copy.103
  104.6 0.5 fusion.19
  105.6 0.6 add_bitcast_fusion
  106.2 0.5 fusion.20
  106.7 0.5 fusion.22
  107.2 0.5 fusion.23
  107.7 0.6 subtract_bitcast_fusion
  108.3 1.4 fusion.52
  109.7 1.4 fusion.50
  111.2 1.5 convolution_add_fusion.1
  112.7 1.8 fusion.15
  114.6 1.1 copy.58
  115.6 45.1 %all_to_all.54 = bf16[2,2,2,64,1024]{4,2,0,1,3:T(2,128)(2,1)S(1)} all-to-all(bf16[2,2,2,64,1024]{4,2,0,1,3:T(2,128)(2,1)S(1)} %copy.58), channel_id=1, replica_groups=mesh['ctx'=64,'ch'=8] {'ctx'}, dimensions={3} | all-to-all | bytes 2097152 | tf_op jit(solution)/shard_map/all_to_all | solution.py:101
  160.7 0.8 copy.59
  161.6 1.5 fusion.209
  165.1 58.0 %all_to_all.55 = bf16[2,64,1,1024]{3,0,2,1:T(2,128)(2,1)S(1)} all-to-all(bf16[2,64,1,1024]{3,0,2,1:T(2,128)(2,1)S(1)} %copy.62), channel_id=1, replica_groups=mesh['ctx'=64,'ch'=8] {'ctx'}, dimensions={1} | all-to-all | bytes 524288 | tf_op jit(solution)/shard_map/all_to_all | solution.py:103
  223.1 20.1 %all-gather.2.cloned.1.call-done = bf16[1024,4096]{0,1:T(8,128)(2,1)} async-done(((bf16[1024,64]{0,1:T(8,128)(2,1)}), bf16[1024,4096]{0,1:T(8,128)(2,1)}) %all-gather.2.cloned.1.call-update) | async-done | bytes 8388624 | tf_op jit(solution)/shard_map/all_gather | solution.py:109
  243.2 7.3 %fusion.2 = bf16[2,64,4096]{2,1,0:T(8,128)(2,1)} fusion(bf16[1024,4096]{0,1:T(8,128)(2,1)} %all-gather.2.cloned.1.call-done, bf16[2,64,1024]{2,1,0:T(8,128)(2,1)S(1)} %copy-done, bf16[2,64,1,1024]{3,0,2,1:T(2,128)(2,1)S(1)} %all_to_all.55), kind=kOutput, calls=%fused_computation.2 | convolution fusion | flops 1074790400 | bytes 9961472 | tf_op jit(solution)/shard_map/sjc,co->sjo/dot_general | solution.py:106
  250.5 39.7 %reduce-scatter.2.cloned.1.call-done = bf16[2,64,512]{2,1,0:T(8,128)(2,1)} async-done(((bf16[2,64,4096]{2,1,0:T(8,128)(2,1)}), bf16[2,64,512]{2,1,0:T(8,128)(2,1)}) %reduce-scatter.2.cloned.1.call-update) | async-done | bytes 131088 | tf_op jit(solution)/shard_map/reduce_scatter | solution.py:112
  (19 shorter events, 3.6 us)
Async XLA Ops:
  6.5 236.6 %all-gather.2.cloned.1.call-start = ((), (), s32[]{:S(2)}) async-start(), calls=%async_computation.5 | async-start | bytes 8519680 | tf_op jit(solution)/shard_map/all_gather | solution.py:109
  10.5 37.8 %all-to-all-start = ((bf16[3,1,64,1024]{3,0,1,2:T(4,128)(2,1)}), bf16[3,1,64,1024]{3,0,1,2:T(4,128)(2,1)S(1)}, u32[]{:S(2)}, u32[]{:S(2)}) async-start(bf16[3,1,64,1024]{3,0,1,2:T(4,128)(2,1)} %copy.53), calls=%async_computation | async-start | bytes 1048576 | tf_op jit(solution)/shard_map/all_to_all | solution.py:97
  54.0 49.7 %all-to-all-start.1 = ((bf16[3,2,128,1,1024]{4,1,3,0,2:T(2,128)(2,1)}), bf16[3,2,128,1,1024]{4,1,3,0,2:T(2,128)(2,1)S(1)}, u32[]{:S(2)}, u32[]{:S(2)}) async-start(bf16[3,2,128,1,1024]{4,1,3,0,2:T(2,128)(2,1)} %copy.55), calls=%async_computation.1 | async-start | bytes 3145728 | tf_op jit(solution)/shard_map/all_to_all | solution.py:99
  63.8 226.4 %reduce-scatter.2.cloned.1.call-start = ((), (), s32[]{:S(2)}) async-start(), calls=%async_computation.6 | async-start | bytes 1179648 | tf_op jit(solution)/shard_map/reduce_scatter | solution.py:112
  164.3 78.8 %copy-start = (bf16[2,64,1024]{2,1,0:T(8,128)(2,1)S(1)}, bf16[2,64,1024]{2,1,0:T(8,128)(2,1)}, u32[]{:S(2)}) copy-start(bf16[2,64,1024]{2,1,0:T(8,128)(2,1)} %param.5) | copy-start | bytes 786436
Sparse Core Ops, SparseCore 0:
  11.8 231.3 all-gather.1
  250.6 39.5 reduce-scatter.1
where the time goes:
time: 297 us
  waiting for transfers between devices  119 us (40%)
  blocking collectives  103 us (35%)
  starting transfers between devices  29.2 us (10%)
  matrix products  21.6 us (7%)
  between operations  13.6 us (5%)
  local copies, waits for them, and re-layouts  8.48 us (3%)
    all_to_all x1, blocking collectives, on_device(): lax.all_to_all(convolved, 'ctx', split_axis=1, concat_axis=2, tiled=True)  58 us
    all_to_all x1, blocking collectives, on_device(): lax.all_to_all(back_pair, 'ctx', split_axis=3, concat_axis=2, tiled=True)  45.1 us
    reduce_scatter x1, waiting for transfers between devices, on_device(): lax.psum_scatter(partial_value.astype(jnp.bfloat16), 'ch', scatter_dimens...  39.7 us
    all_to_all x1, waiting for transfers between devices, on_device(): lax.all_to_all(first, 'ctx', split_axis=2, concat_axis=3, tiled=True)  39.5 us
    all_gather x1, waiting for transfers between devices, on_device(): lax.all_gather(out_weight, 'ctx', axis=1, tiled=True)  20.1 us
    all_to_all x1, starting transfers between devices, on_device(): lax.all_to_all(stacked, 'ctx', split_axis=2, concat_axis=1, tiled=True)  19.1 us
    all_to_all x1, waiting for transfers between devices, on_device(): lax.all_to_all(stacked, 'ctx', split_axis=2, concat_axis=1, tiled=True)  18.6 us
    all_to_all x1, starting transfers between devices, on_device(): lax.all_to_all(first, 'ctx', split_axis=2, concat_axis=3, tiled=True)  9.84 us
  transfers between devices with their start and end apart: 4, of which 4 were waited for; matrix products, arithmetic and copies ran while one was open for 8% of the time, Pallas kernels for 0%

commit v1 on v0

v1 whole, which is shorter than its diff:
```python
import functools
import math

import jax
import jax.numpy as jnp
import numpy as np
from jax import lax
from jax.experimental import pallas as pl
from jax.experimental.pallas import tpu as pltpu
from jax.sharding import PartitionSpec as P

MESH = pl.DeviceIdType.MESH
F32 = jnp.float32
BF16 = jnp.bfloat16


def tables():
    n1, n2, span = 128, 64, 8192
    k1 = np.arange(n1)
    b = np.arange(64)
    j = np.arange(n2)
    th = 2 * math.pi * ((k1[:, None] * b[None, :]) % n1) / n1
    cs = np.concatenate([np.cos(th), np.sin(th)], 1)
    ph = 2 * math.pi * ((k1[:, None] * j[None, :]) % span) / span
    c, s = np.cos(ph), np.sin(ph)
    tc = np.concatenate([c, c], 1)
    ts = np.concatenate([s, -s], 1)
    tcn = np.concatenate([-c, c], 1)
    tsn = np.concatenate([-s, -s], 1)
    twid = np.stack([tc, ts, tcn, tsn])
    t2 = 2 * math.pi * ((j[:, None] * j[None, :]) % n2) / n2
    c2, s2 = np.cos(t2), np.sin(t2)
    fwd = np.block([[c2, -s2, -s2, c2], [s2, c2, c2, s2]])
    filt = np.block([[c2, c2, s2, -s2], [s2, s2, -c2, c2]])
    inv = np.block([[c2, s2, s2, c2], [-s2, c2, c2, -s2]])
    mid = np.stack([fwd, filt, inv])
    last = np.concatenate([np.cos(th.T), np.sin(th.T)], 1) / span
    return (
        jnp.asarray(cs, BF16),
        jnp.asarray(twid, F32),
        jnp.asarray(mid, BF16),
        jnp.asarray(last, BF16),
    )


def kernel(
    pre_h, sig_h, fil_h, post_h, w_h, cs_h, tw_h, mid_h, last_h,
    out,
    pre, sig, fil, post, w, cs, tw, mid, last,
    msg1, rcv1, xf, of, msg2, rcv2, post_t, post_r, lhs, wall, half, rcv3, own, summ, rcv4,
    in_sem, s1, r1, wy_s, wy_r, wz_s, wz_r, ps, pr, s2, r2, gs, gr, es, er, fs, fr,
):
    me = lax.axis_index("ctx")
    ch = lax.axis_index("ch")
    x = lax.rem(me, 4)
    zy = me // 4
    h = lax.rem(zy, 2)
    z = zy // 2
    core = lax.rem(ch, 2)
    yl = ch // 2

    loads = []
    for i, (src, dst) in enumerate(
        [(pre_h, pre), (sig_h, sig), (fil_h, fil), (w_h, w), (post_h, post),
         (cs_h, cs), (tw_h, tw), (mid_h, mid), (last_h, last)]
    ):
        cp = pltpu.make_async_copy(src, dst, in_sem.at[i])
        cp.start()
        loads.append(cp)

    barrier = pltpu.get_barrier_semaphore()

    def greet(k, carry):
        pl.semaphore_signal(barrier, inc=1, device_id=(lax.rem(me + k, 64), ch), device_id_type=MESH)
        return carry

    lax.fori_loop(1, 64, greet, 0)

    def greet2(k, carry):
        px = lax.rem(x + lax.rem(k, 4), 4)
        py = lax.rem(yl + k // 4, 4)
        pl.semaphore_signal(
            barrier, inc=1, device_id=(zy * 4 + px, py * 2 + core), device_id_type=MESH
        )
        return carry

    lax.fori_loop(4, 16, greet2, 0)
    pl.semaphore_signal(barrier, inc=1, device_id=(me, yl * 2 + 1 - core), device_id_type=MESH)

    low = lax.broadcasted_iota(jnp.int32, (8, 128), 1) < 64

    for i in range(3):
        loads[i].wait()
    for blk in range(8):
        lanes = slice(128 * blk, 128 * blk + 128)
        v = [
            (pre[s, :, lanes].astype(F32) * sig[s, :, lanes].astype(F32)).astype(BF16).astype(F32)
            for s in range(2)
        ]
        xt = jnp.concatenate(v, 0).T
        f = fil[:, lanes].astype(F32)
        ft = jnp.concatenate([f, f], 0).T
        for i in range(8):
            q = 8 * blk + i
            msg1[q, 0:16, :] = xt[16 * i : 16 * i + 16].astype(BF16)
            msg1[q, 16:24, :] = jnp.where(
                low, ft[16 * i : 16 * i + 8], ft[16 * i + 8 : 16 * i + 16]
            ).astype(BF16)

    pl.semaphore_wait(barrier, 76)

    def send1(k, carry):
        to = lax.rem(me + k, 64)
        q = lax.rem(to, 4) * 16 + to // 4
        pltpu.make_async_remote_copy(
            src_ref=msg1.at[q], dst_ref=rcv1.at[me], send_sem=s1, recv_sem=r1,
            device_id=(to, ch), device_id_type=MESH,
        ).start()
        return carry

    lax.fori_loop(1, 64, send1, 0)
    rcv1[me] = msg1[x * 16 + zy]

    loads[3].wait()
    for blk in range(8):
        wb = w[128 * blk : 128 * blk + 128, :].astype(F32)
        wall[zy, :, 128 * blk : 128 * blk + 128] = wb.T.astype(BF16)
    wy = pltpu.make_async_remote_copy(
        src_ref=wall.at[zy], dst_ref=wall.at[zy], send_sem=wy_s, recv_sem=wy_r,
        device_id=((zy + 1 - 2 * h) * 4 + x, ch), device_id_type=MESH,
    )
    wy.start()

    loads[4].wait()
    for blk in range(8):
        lanes = slice(128 * blk, 128 * blk + 128)
        pt = jnp.concatenate([post[s, :, lanes].astype(F32) for s in range(2)], 0).T
        for i in range(8):
            post_t[8 * blk + i] = pt[16 * i : 16 * i + 16].astype(BF16)

    def post_copy(d):
        px = lax.rem(x + d, 4)
        return pltpu.make_async_remote_copy(
            src_ref=post_t.at[pl.ds(16 * px, 16)], dst_ref=post_r.at[x], send_sem=ps, recv_sem=pr,
            device_id=(zy * 4 + px, ch), device_id_type=MESH,
        )

    for d in range(1, 4):
        post_copy(d).start()
    post_r[x] = post_t[pl.ds(16 * x, 16)]

    def ring(step):
        right_z, left_z = lax.rem(z + 1, 8), lax.rem(z + 7, 8)
        pair_r = lax.rem(z + 8 - step + 1, 8)
        pair_l = lax.rem(z + step - 1, 8)
        if step < 4:
            part_r, part_l = pl.ds(2 * pair_r, 2), pl.ds(2 * pair_l, 2)
        else:
            part_r, part_l = pl.ds(2 * pair_r, 1), pl.ds(2 * pair_l + 1, 1)
        to_right = pltpu.make_async_remote_copy(
            src_ref=wall.at[part_r], dst_ref=wall.at[part_r],
            send_sem=wz_s.at[2 * step - 2], recv_sem=wz_r.at[2 * step - 2],
            device_id=((right_z * 2 + h) * 4 + x, ch), device_id_type=MESH,
        )
        to_left = pltpu.make_async_remote_copy(
            src_ref=wall.at[part_l], dst_ref=wall.at[part_l],
            send_sem=wz_s.at[2 * step - 1], recv_sem=wz_r.at[2 * step - 1],
            device_id=((left_z * 2 + h) * 4 + x, ch), device_id_type=MESH,
        )
        return to_right, to_left

    rings = [ring(i) for i in range(1, 5)]
    wy.wait_recv()
    for cp in rings[0]:
        cp.start()

    for i in range(5, 9):
        loads[i].wait()
    pltpu.make_async_remote_copy(
        src_ref=msg1.at[pl.ds(0, 63)], dst_ref=rcv1.at[pl.ds(0, 63)], send_sem=s1, recv_sem=r1,
        device_id=(me, ch), device_id_type=MESH,
    ).wait_recv()

    def widen(b, carry):
        xf[pl.ds(pl.multiple_of(b * 24, 8), 24), :] = rcv1[b].astype(F32)
        return carry

    lax.fori_loop(0, 64, widen, 0, unroll=8)

    for cp in rings[0]:
        cp.wait_recv()
    for cp in rings[1]:
        cp.start()

    wide_low = lax.broadcasted_iota(jnp.int32, (64, 128), 1) < 64
    sign = jnp.where(wide_low, 1.0, -1.0).astype(F32)
    zero = jnp.zeros((64, 128), F32)

    def pair(c, carry):
        g = xf[pl.ds(16 + c, 64, stride=24), :]
        rg = pltpu.roll(g, 64, 1)
        for part in range(2):
            v = xf[pl.ds(c + 8 * part, 64, stride=24), :]
            r = pltpu.roll(v, 64, 1)
            own_h, oth_h = (g, rg) if part == 0 else (rg, g)
            lo = jnp.where(wide_low, own_h, zero)
            hi = jnp.where(wide_low, zero, oth_h)
            top = jnp.concatenate([v, r, lo, hi], 1).astype(BF16)
            bot = jnp.concatenate([r * sign, -v * sign, -hi, -lo], 1).astype(BF16)
            a = jnp.dot(cs[...], jnp.concatenate([top, bot], 0), preferred_element_type=F32)
            tc, ts = tw[0], tw[1]
            sg = (a[:, 0:128] * tc + a[:, 128:256] * ts).astype(BF16)
            fg = (a[:, 256:384] * tc + a[:, 384:512] * ts).astype(BF16)
            zz = jnp.dot(sg, mid[0], preferred_element_type=F32)
            hh = jnp.dot(fg, mid[1], preferred_element_type=F32)
            p = (zz[:, 0:128] * hh[:, 0:128] + zz[:, 128:256] * hh[:, 128:256]).astype(BF16)
            m = jnp.dot(p, mid[2], preferred_element_type=F32)
            m0, m1 = m[:, 0:128], m[:, 128:256]
            back = jnp.concatenate(
                [(m0 * tc - m1 * ts).astype(BF16), (m1 * tw[2] + m0 * tw[3]).astype(BF16)], 0
            )
            of[pl.ds(c + 8 * part, 64, stride=16), :] = jnp.dot(
                last[...], back, preferred_element_type=F32
            )
        return carry

    lax.fori_loop(0, 4, pair, 0)
    for cp in rings[1]:
        cp.wait_recv()
    for cp in rings[2]:
        cp.start()
    lax.fori_loop(4, 8, pair, 0)

    def narrow(b, carry):
        msg2[b] = of[pl.ds(pl.multiple_of(b * 16, 16), 16), :].astype(BF16)
        return carry

    lax.fori_loop(0, 64, narrow, 0, unroll=8)

    def send2(k, carry):
        to = lax.rem(zy + k, 16)
        pltpu.make_async_remote_copy(
            src_ref=msg2.at[pl.ds(4 * to, 4)], dst_ref=rcv2.at[zy], send_sem=s2, recv_sem=r2,
            device_id=(to * 4 + x, ch), device_id_type=MESH,
        ).start()
        return carry

    lax.fori_loop(1, 16, send2, 0)
    rcv2[zy] = msg2[pl.ds(4 * zy, 4)]

    pltpu.make_async_remote_copy(
        src_ref=post_r.at[pl.ds(0, 3)], dst_ref=post_r.at[pl.ds(0, 3)], send_sem=ps, recv_sem=pr,
        device_id=(me, ch), device_id_type=MESH,
    ).wait_recv()
    for cp in rings[2]:
        cp.wait_recv()
    for cp in rings[3]:
        cp.start()
    pltpu.make_async_remote_copy(
        src_ref=rcv2.at[pl.ds(0, 15)], dst_ref=rcv2.at[pl.ds(0, 15)], send_sem=s2, recv_sem=r2,
        device_id=(me, ch), device_id_type=MESH,
    ).wait_recv()

    for px in range(4):
        gt = (rcv2[:, px].astype(F32) * post_r[px].astype(F32)).astype(BF16).astype(F32)
        gt = gt.reshape(256, 128)
        for i in range(2):
            lhs[
                128 * px : 128 * px + 128,
                pl.ds(pl.multiple_of(256 * x + 128 * i, 128), 128),
            ] = gt[128 * i : 128 * i + 128].T.astype(BF16)

    def gather(d):
        px = lax.rem(x + d, 4)
        mine = lhs.at[:, pl.ds(pl.multiple_of(256 * x, 256), 256)]
        return pltpu.make_async_remote_copy(
            src_ref=mine, dst_ref=mine, send_sem=gs.at[d - 1], recv_sem=gr.at[d - 1],
            device_id=(zy * 4 + px, ch), device_id_type=MESH,
        )

    gathers = [gather(d) for d in range(1, 4)]
    for cp in gathers:
        cp.start()
    for cp in rings[3]:
        cp.wait_recv()
    for cp in gathers:
        cp.wait_recv()

    sib = (me, yl * 2 + 1 - core)

    def swap(y):
        return pltpu.make_async_remote_copy(
            src_ref=half.at[y], dst_ref=rcv3.at[y], send_sem=es.at[y], recv_sem=er.at[y],
            device_id=sib, device_id_type=MESH,
        )

    def columns(y, c):
        return wall[pl.ds(4 * y + 2 * c, 2)].reshape(128, 1024)

    dims = (((1,), (1,)), ((), ()))
    for yp in range(2):
        wt = jnp.concatenate([columns(2 * yp, 1 - core), columns(2 * yp + 1, 1 - core)], 0)
        acc = lax.dot_general(lhs[...], wt, dims, preferred_element_type=F32)
        half[2 * yp] = acc[:, 0:128].astype(BF16)
        half[2 * yp + 1] = acc[:, 128:256].astype(BF16)
        swap(2 * yp).start()
        swap(2 * yp + 1).start()
    for yp in range(2):
        wt = jnp.concatenate([columns(2 * yp, core), columns(2 * yp + 1, core)], 0)
        acc = lax.dot_general(lhs[...], wt, dims, preferred_element_type=F32)
        own[2 * yp] = acc[:, 0:128]
        own[2 * yp + 1] = acc[:, 128:256]

    for y in range(4):
        swap(y).wait_recv()
        summ[y] = (own[y] + rcv3[y].astype(F32)).astype(BF16)

    def last_send(k, carry):
        px = lax.rem(x + lax.rem(k, 4), 4)
        py = lax.rem(yl + k // 4, 4)
        pltpu.make_async_remote_copy(
            src_ref=summ.at[py, pl.ds(pl.multiple_of(128 * px, 128), 128)],
            dst_ref=rcv4.at[x * 4 + yl], send_sem=fs, recv_sem=fr,
            device_id=(zy * 4 + px, py * 2 + core), device_id_type=MESH,
        ).start()
        return carry

    lax.fori_loop(1, 16, last_send, 0)
    rcv4[x * 4 + yl] = summ[yl, pl.ds(pl.multiple_of(128 * x, 128), 128)]
    pltpu.make_async_remote_copy(
        src_ref=rcv4.at[pl.ds(0, 15)], dst_ref=rcv4.at[pl.ds(0, 15)], send_sem=fs, recv_sem=fr,
        device_id=(me, ch), device_id_type=MESH,
    ).wait_recv()

    t = []
    for px in range(4):
        v = rcv4[4 * px].astype(F32)
        for y in range(1, 4):
            v = v + rcv4[4 * px + y].astype(F32)
        t.append(v)
    row_low = lax.broadcasted_iota(jnp.int32, (128, 128), 1) < 64
    for m in range(4):
        a, b = t[(2 * m) % 4], t[(2 * m + 1) % 4]
        if m < 2:
            o = jnp.where(row_low, a, pltpu.roll(b, 64, 1))
        else:
            o = jnp.where(row_low, pltpu.roll(a, 64, 1), b)
        o = o.astype(BF16)
        out[0, :, 128 * m : 128 * m + 128] = o[0:64]
        out[1, :, 128 * m : 128 * m + 128] = o[64:128]

    pltpu.make_async_remote_copy(
        src_ref=msg1.at[pl.ds(0, 63)], dst_ref=rcv1.at[pl.ds(0, 63)], send_sem=s1, recv_sem=r1,
        device_id=(me, ch), device_id_type=MESH,
    ).wait_send()
    wy.wait_send()
    for pr_ in rings:
        for cp in pr_:
            cp.wait_send()
    pltpu.make_async_remote_copy(
        src_ref=post_r.at[pl.ds(0, 3)], dst_ref=post_r.at[pl.ds(0, 3)], send_sem=ps, recv_sem=pr,
        device_id=(me, ch), device_id_type=MESH,
    ).wait_send()
    pltpu.make_async_remote_copy(
        src_ref=rcv2.at[pl.ds(0, 15)], dst_ref=rcv2.at[pl.ds(0, 15)], send_sem=s2, recv_sem=r2,
        device_id=(me, ch), device_id_type=MESH,
    ).wait_send()
    for cp in gathers:
        cp.wait_send()
    for y in range(4):
        swap(y).wait_send()
    pltpu.make_async_remote_copy(
        src_ref=rcv4.at[pl.ds(0, 15)], dst_ref=rcv4.at[pl.ds(0, 15)], send_sem=fs, recv_sem=fr,
        device_id=(me, ch), device_id_type=MESH,
    ).wait_send()


def on_device(post_gate, pre_gate, signal, long_filter, out_weight):
    cs, tw, mid, last = tables()
    vm = pltpu.VMEM
    dma = pltpu.SemaphoreType.DMA
    scratch = [
        vm((2, 64, 1024), BF16), vm((2, 64, 1024), BF16), vm((64, 1024), BF16),
        vm((2, 64, 1024), BF16), vm((1024, 64), BF16),
        vm((128, 128), BF16), vm((4, 128, 128), F32), vm((3, 128, 256), BF16), vm((64, 256), BF16),
        vm((64, 24, 128), BF16),
        vm((64, 24, 128), BF16),
        vm((1536, 128), F32),
        vm((1024, 128), F32),
        vm((64, 16, 128), BF16),
        vm((16, 4, 16, 128), BF16),
        vm((64, 16, 128), BF16),
        vm((4, 16, 16, 128), BF16),
        vm((512, 1024), BF16),
        vm((16, 64, 1024), BF16),
        vm((4, 512, 128), BF16),
        vm((4, 512, 128), BF16),
        vm((4, 512, 128), F32),
        vm((4, 512, 128), BF16),
        vm((16, 128, 128), BF16),
        dma((9,)), dma, dma, dma, dma, dma((8,)), dma((8,)), dma, dma, dma, dma,
        dma((3,)), dma((3,)), dma((4,)), dma((4,)), dma, dma,
    ]
    return pl.pallas_call(
        kernel,
        out_shape=jax.ShapeDtypeStruct((2, 64, 512), BF16),
        in_specs=[pl.BlockSpec(memory_space=pl.ANY)] * 9,
        out_specs=pl.BlockSpec(memory_space=pltpu.VMEM),
        scratch_shapes=scratch,
        compiler_params=pltpu.CompilerParams(
            collective_id=0, has_side_effects=True, vmem_limit_bytes=40 * 1024 * 1024
        ),
        cost_estimate=pl.CostEstimate(flops=2_000_000_000, bytes_accessed=4_000_000, transcendentals=0),
    )(pre_gate, signal, long_filter, post_gate, out_weight, cs, tw, mid, last)


def solution(mesh):
    return jax.shard_map(
        on_device,
        mesh=mesh,
        in_specs=(
            P(None, "ctx", "ch"),
            P(None, "ctx", "ch"),
            P(None, "ctx", "ch"),
            P("ctx", "ch"),
            P("ch", "ctx"),
        ),
        out_specs=P(None, "ctx", "ch"),
        check_vma=False,
    )
```

time: 297 us -> 98.7 us (0.33)
  the two profiles are of different devices: /device:TPU:4 before, /device:TPU:25 now
where the time goes in v1:
time: 98.7 us; the launch traced here: 98.3 us
  Pallas kernels  91.2 us (92%)
  local copies, waits for them, and re-layouts  7.07 us (7%)
    pallas_call x1, Pallas kernels, on_device(): pl.pallas_call(kernel, out_shape=jax.ShapeDtypeStruct((2, 64, 512), BF16)...  91.2 us
    unnamed x18, local copies, waits for them, and re-layouts  7.07 us

profile of v1, /device:TPU:25, one launch (start us, length us, event | category | flops | bytes accessed | tf_op | source)
XLA Modules:
  0.0 98.3 jit_solution(15575675995076806876)
XLA Ops:
  0.0 0.0 copy-start.3
  0.0 0.0 copy-start
  0.0 1.1 %copy.10.w_h = bf16[1024,64]{1,0:T(8,128)(2,1)S(1)} copy(bf16[1024,64]{0,1:T(8,128)(2,1)} %param.13) | data formatting | bytes 262144 | tf_op args[4]
  1.1 0.0 copy-done.3
  1.1 0.0 copy-done
  1.2 0.0 copy-start.1
  1.2 0.9 copy-done.1
  2.1 0.0 copy-start.2
  2.1 0.9 copy-done.2
  3.1 0.0 copy-start.4
  3.1 0.9 copy-done.4
  4.0 0.0 copy-start.5
  4.0 0.9 copy-done.5
  4.9 0.0 copy-start.6
  4.9 0.8 copy-done.6
  5.7 0.0 copy-start.7
  5.7 0.8 copy-done.7
  6.5 91.2 %shard_map.91 = bf16[2,64,512]{2,1,0:T(8,128)(2,1)S(1)} custom-call(bf16[2,64,1024]{2,1,0:T(8,128)(2,1)S(1)} %copy-done, bf16[2,64,1024]{2,1,0:T(8,128)(2,1)S(1)} %copy-done.1, bf16[64,1024]{1,0:T(8,128)(2,1)S(1)} %copy-done.3, bf16[2,64,1024]{2,1,0:T(8,128)(2,1)S(1)} %copy-done.2, bf16[1024,64]{1,0:T(8,128)(2,1)S(1)} %copy.10.w_h, ...), custom_call_target="tpu_custom_call" | custom-call | flops 2000000000 | bytes 4000000 | tf_op jit(solution)/shard_map/pallas_call | solution.py:404
  97.7 0.7 copy.12
Async XLA Ops:
  0.0 1.1 %copy-start.3 = (bf16[64,1024]{1,0:T(8,128)(2,1)S(1)}, bf16[64,1024]{1,0:T(8,128)(2,1)}, u32[]{:S(2)}) copy-start(bf16[64,1024]{1,0:T(8,128)(2,1)} %fil_h.1) | copy-start | bytes 393220
  0.0 1.1 %copy-start = (bf16[2,64,1024]{2,1,0:T(8,128)(2,1)S(1)}, bf16[2,64,1024]{2,1,0:T(8,128)(2,1)}, u32[]{:S(2)}) copy-start(bf16[2,64,1024]{2,1,0:T(8,128)(2,1)} %pre_h.1) | copy-start | bytes 786436
  1.2 1.0 copy-start.1
  2.1 0.9 copy-start.2
  3.1 0.9 copy-start.4
  4.0 0.9 copy-start.5
  4.9 0.8 copy-start.6
  5.7 0.8 copy-start.7

commit v2 on v0

v2 whole, which is shorter than its diff:
```python
import functools
import math

import jax
import jax.numpy as jnp
import numpy as np
from jax import lax
from jax.experimental import pallas as pl
from jax.experimental.pallas import tpu as pltpu
from jax.sharding import PartitionSpec as P

WT, POST = True, True
PLAN = {"scatter1": ("a1",), "filter0": ("a2",), "back0": ("b1",), "recv1": ("a3",), "back1": ("b2", "a4"), "gather0": ("b3",), "gather1": ("b4", "a5"), "matmul": ("b5",)}
WY_FIRST = False
MESH = pl.DeviceIdType.MESH
F32 = jnp.float32
BF16 = jnp.bfloat16


def tables():
    n1, n2, span = 128, 64, 8192
    k1 = np.arange(n1)
    b = np.arange(64)
    j = np.arange(n2)
    th = 2 * math.pi * ((k1[:, None] * b[None, :]) % n1) / n1
    cs = np.concatenate([np.cos(th), np.sin(th)], 1)
    ph = 2 * math.pi * ((k1[:, None] * j[None, :]) % span) / span
    c, s = np.cos(ph), np.sin(ph)
    tc = np.concatenate([c, c], 1)
    ts = np.concatenate([s, -s], 1)
    tcn = np.concatenate([-c, c], 1)
    tsn = np.concatenate([-s, -s], 1)
    twid = np.stack([tc, ts, tcn, tsn])
    t2 = 2 * math.pi * ((j[:, None] * j[None, :]) % n2) / n2
    c2, s2 = np.cos(t2), np.sin(t2)
    fwd = np.block([[c2, -s2, -s2, c2], [s2, c2, c2, s2]])
    filt = np.block([[c2, c2, s2, -s2], [s2, s2, -c2, c2]])
    inv = np.block([[c2, s2, s2, c2], [-s2, c2, c2, -s2]])
    mid = np.stack([fwd, filt, inv])
    last = np.concatenate([np.cos(th.T), np.sin(th.T)], 1) / span
    return (
        jnp.asarray(cs, BF16),
        jnp.asarray(twid, F32),
        jnp.asarray(mid, BF16),
        jnp.asarray(last, BF16),
    )


def kernel(
    pre_h, sig_h, fil_h, post_h, w_h, cs_h, tw_h, mid_h, last_h,
    out,
    pre, sig, fil, post, cs, tw, mid, last,
    msg_a, rcv_a, msg_b, rcv_b, xa, xb, hf, st1, st2, st3, of, msg2, rcv2, post_t, post_r,
    lhs, wall, half, rcv3, own, summ, rcv4,
    in_sem, s1, r1, wy_s, wy_r, wa_s, wa_r, wb_s, wb_r, ps, pr, s2, r2, gs, gr, es, er, fs, fr,
):
    me = lax.axis_index("ctx")
    ch = lax.axis_index("ch")
    x = lax.rem(me, 4)
    zy = me // 4
    h = lax.rem(zy, 2)
    z = zy // 2
    core = lax.rem(ch, 2)
    yl = ch // 2
    slot = x * 16 + zy

    loads = []
    for i, (src, dst) in enumerate(
        [(pre_h, pre), (sig_h, sig), (fil_h, fil), (w_h, wall.at[zy]), (post_h, post),
         (cs_h, cs), (tw_h, tw), (mid_h, mid), (last_h, last)]
    ):
        cp = pltpu.make_async_copy(src, dst, in_sem.at[i])
        cp.start()
        loads.append(cp)

    barrier = pltpu.get_barrier_semaphore()

    def greet(k, carry):
        pl.semaphore_signal(barrier, inc=1, device_id=(lax.rem(me + k, 64), ch), device_id_type=MESH)
        return carry

    lax.fori_loop(1, 64, greet, 0)

    def greet2(k, carry):
        px = lax.rem(x + lax.rem(k, 4), 4)
        py = lax.rem(yl + k // 4, 4)
        pl.semaphore_signal(
            barrier, inc=1, device_id=(zy * 4 + px, py * 2 + core), device_id_type=MESH
        )
        return carry

    lax.fori_loop(4, 16, greet2, 0)
    pl.semaphore_signal(barrier, inc=1, device_id=(me, yl * 2 + 1 - core), device_id_type=MESH)

    low = lax.broadcasted_iota(jnp.int32, (8, 128), 1) < 64

    for i in range(3):
        loads[i].wait()
    for px in range(4):
        fts = []
        for c in range(2):
            lanes = slice(256 * px + 128 * c, 256 * px + 128 * c + 128)
            v = [
                (pre[s, :, lanes].astype(F32) * sig[s, :, lanes].astype(F32)).astype(BF16).astype(F32)
                for s in range(2)
            ]
            xt = jnp.concatenate(v, 0).T
            dst = (msg_a, msg_b)[c]
            for i in range(16):
                dst[16 * px + i, 0:8, :] = xt[8 * i : 8 * i + 8].astype(BF16)
            f = fil[:, lanes].astype(F32)
            fts.append(jnp.concatenate([f, f], 0).T)
        for i in range(16):
            msg_a[16 * px + i, 8:16, :] = jnp.where(
                low, fts[0][8 * i : 8 * i + 8], fts[1][8 * i : 8 * i + 8]
            ).astype(BF16)

    pl.semaphore_wait(barrier, 76)

    msgs, rcvs = (msg_a, msg_b), (rcv_a, rcv_b)

    def all1(c):
        return pltpu.make_async_remote_copy(
            src_ref=msgs[c].at[pl.ds(0, 63)], dst_ref=rcvs[c].at[pl.ds(0, 63)],
            send_sem=s1.at[c], recv_sem=r1.at[c], device_id=(me, ch), device_id_type=MESH,
        )

    def scatter(c):
        def send1(k, carry):
            to = lax.rem(me + k, 64)
            pltpu.make_async_remote_copy(
                src_ref=msgs[c].at[lax.rem(to, 4) * 16 + to // 4], dst_ref=rcvs[c].at[me],
                send_sem=s1.at[c], recv_sem=r1.at[c], device_id=(to, ch), device_id_type=MESH,
            ).start()
            return carry

        lax.fori_loop(1, 64, send1, 0)
        rcvs[c][me] = msgs[c][slot]

    wy = pltpu.make_async_remote_copy(
        src_ref=wall.at[zy], dst_ref=wall.at[zy], send_sem=wy_s, recv_sem=wy_r,
        device_id=((zy + 1 - 2 * h) * 4 + x, ch), device_id_type=MESH,
    )

    def ring(step, hh, ssem, rsem):
        right_z, left_z = lax.rem(z + 1, 8), lax.rem(z + 7, 8)
        from_r = 2 * lax.rem(z + 9 - step, 8) + hh
        from_l = 2 * lax.rem(z + step - 1, 8) + hh
        if step < 4:
            part_r, part_l = wall.at[from_r], wall.at[from_l]
        else:
            part_r, part_l = wall.at[from_r, pl.ds(0, 32)], wall.at[from_l, pl.ds(32, 32)]
        return [
            pltpu.make_async_remote_copy(
                src_ref=part, dst_ref=part,
                send_sem=ssem.at[2 * step - 2 + i], recv_sem=rsem.at[2 * step - 2 + i],
                device_id=((to * 2 + h) * 4 + x, ch), device_id_type=MESH,
            )
            for i, (part, to) in enumerate([(part_r, right_z), (part_l, left_z)])
        ]

    ring_a = [ring(i, h, wa_s, wa_r) for i in range(1, 5)]
    ring_b = [ring(i, 1 - h, wb_s, wb_r) for i in range(1, 5)]

    def step_w(which, i):
        if not WT:
            return
        rings = ring_a if which == "a" else ring_b
        if i > 1:
            for cp in rings[i - 2]:
                cp.wait_recv()
        elif which == "b":
            wy.wait_recv()
        if i < 5:
            for cp in rings[i - 1]:
                cp.start()

    def at(name):
        for op in PLAN.get(name, ()):
            step_w(op[0], int(op[1]))

    loads[3].wait()
    if WT and WY_FIRST:
        wy.start()
    scatter(0)
    at("scatter0")
    scatter(1)
    if WT and not WY_FIRST:
        wy.start()
    at("scatter1")

    loads[4].wait()
    for px in range(4):
        for c in range(2):
            lanes = slice(256 * px + 128 * c, 256 * px + 128 * c + 128)
            pt = jnp.concatenate([post[s, :, lanes].astype(F32) for s in range(2)], 0).T
            post_t[px, c] = pt.astype(BF16)

    def post_copy(d):
        px = lax.rem(x + d, 4)
        return pltpu.make_async_remote_copy(
            src_ref=post_t.at[px], dst_ref=post_r.at[x], send_sem=ps, recv_sem=pr,
            device_id=(zy * 4 + px, ch), device_id_type=MESH,
        )

    if POST:
        for d in range(1, 4):
            post_copy(d).start()
    post_r[x] = post_t[x]
    all_post = pltpu.make_async_remote_copy(
        src_ref=post_r.at[pl.ds(0, 3)], dst_ref=post_r.at[pl.ds(0, 3)], send_sem=ps, recv_sem=pr,
        device_id=(me, ch), device_id_type=MESH,
    )
    at("post")

    wide_low = lax.broadcasted_iota(jnp.int32, (64, 128), 1) < 64
    sign = jnp.where(wide_low, 1.0, -1.0).astype(F32)
    zero = jnp.zeros((64, 128), F32)

    def widen_a(b, carry):
        xa[pl.ds(pl.multiple_of(b * 16, 16), 16), :] = rcv_a[b].astype(F32)
        return carry

    def widen_b(b, carry):
        xb[pl.ds(pl.multiple_of(b * 8, 8), 8), :] = rcv_b[b].astype(F32)
        return carry

    def filter_half(c):
        for r in range(8):
            g = xa[pl.ds(8 + r, 64, stride=16), :]
            rg = pltpu.roll(g, 64, 1)
            own_h, oth_h = (g, rg) if c == 0 else (rg, g)
            lo = jnp.where(wide_low, own_h, zero)
            hi = jnp.where(wide_low, zero, oth_h)
            rhs = jnp.concatenate(
                [jnp.concatenate([lo, hi], 1), jnp.concatenate([-hi, -lo], 1)], 0
            ).astype(BF16)
            a = jnp.dot(cs[...], rhs, preferred_element_type=F32)
            st1[128 * r : 128 * r + 128] = (a[:, 0:128] * tw[0] + a[:, 128:256] * tw[1]).astype(BF16)
        for r in range(0, 8, 2):
            rows = slice(128 * r, 128 * r + 256)
            hf[rows, :] = jnp.dot(st1[rows, :], mid[1], preferred_element_type=F32)

    def signal_half(c):
        for r in range(8):
            v = xa[pl.ds(r, 64, stride=16), :] if c == 0 else xb[pl.ds(r, 64, stride=8), :]
            rv = pltpu.roll(v, 64, 1)
            rhs = jnp.concatenate(
                [jnp.concatenate([v, rv], 1), jnp.concatenate([rv * sign, -v * sign], 1)], 0
            ).astype(BF16)
            a = jnp.dot(cs[...], rhs, preferred_element_type=F32)
            st1[128 * r : 128 * r + 128] = (a[:, 0:128] * tw[0] + a[:, 128:256] * tw[1]).astype(BF16)
        for r in range(0, 8, 2):
            rows = slice(128 * r, 128 * r + 256)
            zz = jnp.dot(st1[rows, :], mid[0], preferred_element_type=F32)
            st2[rows, :] = (
                zz[:, 0:128] * hf[rows, 0:128] + zz[:, 128:256] * hf[rows, 128:256]
            ).astype(BF16)
        for r in range(0, 8, 2):
            m = jnp.dot(st2[128 * r : 128 * r + 256, :], mid[2], preferred_element_type=F32)
            for i in range(2):
                m0, m1 = m[128 * i : 128 * i + 128, 0:128], m[128 * i : 128 * i + 128, 128:256]
                at_row = 256 * (r + i)
                st3[at_row : at_row + 128] = (m0 * tw[0] - m1 * tw[1]).astype(BF16)
                st3[at_row + 128 : at_row + 256] = (m1 * tw[2] + m0 * tw[3]).astype(BF16)
        for r in range(8):
            of[pl.ds(r, 64, stride=8), :] = jnp.dot(
                last[...], st3[256 * r : 256 * r + 256], preferred_element_type=F32
            )

        def narrow(b, carry):
            msg2[c, b] = of[pl.ds(pl.multiple_of(b * 8, 8), 8), :].astype(BF16)
            return carry

        lax.fori_loop(0, 64, narrow, 0, unroll=8)

    def all2(c):
        return pltpu.make_async_remote_copy(
            src_ref=rcv2.at[c, pl.ds(0, 15)], dst_ref=rcv2.at[c, pl.ds(0, 15)],
            send_sem=s2.at[c], recv_sem=r2.at[c], device_id=(me, ch), device_id_type=MESH,
        )

    def give_back(c):
        def send2(k, carry):
            to = lax.rem(zy + k, 16)
            pltpu.make_async_remote_copy(
                src_ref=msg2.at[c, pl.ds(4 * to, 4)], dst_ref=rcv2.at[c, zy],
                send_sem=s2.at[c], recv_sem=r2.at[c], device_id=(to * 4 + x, ch), device_id_type=MESH,
            ).start()
            return carry

        lax.fori_loop(1, 16, send2, 0)
        rcv2[c, zy] = msg2[c, pl.ds(4 * zy, 4)]

    for i in range(5, 9):
        loads[i].wait()
    all1(0).wait_recv()
    at("recv0")
    lax.fori_loop(0, 64, widen_a, 0, unroll=8)
    filter_half(0)
    at("filter0")
    signal_half(0)
    give_back(0)
    at("back0")
    filter_half(1)
    at("filter1")
    all1(1).wait_recv()
    at("recv1")
    lax.fori_loop(0, 64, widen_b, 0, unroll=8)
    signal_half(1)
    give_back(1)
    at("back1")

    def gather(c, d):
        px = lax.rem(x + d, 4)
        mine = lhs.at[2 * x + c]
        return pltpu.make_async_remote_copy(
            src_ref=mine, dst_ref=mine, send_sem=gs.at[3 * c + d - 1], recv_sem=gr.at[3 * c + d - 1],
            device_id=(zy * 4 + px, ch), device_id_type=MESH,
        )

    gathers = [[gather(c, d) for d in range(1, 4)] for c in range(2)]
    if POST:
        all_post.wait_recv()
    for c in range(2):
        all2(c).wait_recv()
        at("ret%d" % c)
        for px in range(4):
            gt = rcv2[c, :, px].astype(F32).reshape(128, 128) * post_r[px, c].astype(F32)
            lhs[2 * x + c, 128 * px : 128 * px + 128, :] = gt.astype(BF16).astype(F32).T.astype(BF16)
        for cp in gathers[c]:
            cp.start()
        at("gather%d" % c)
    for c in range(2):
        for cp in gathers[c]:
            cp.wait_recv()
    at("matmul")

    def swap(dy):
        return pltpu.make_async_remote_copy(
            src_ref=half.at[dy], dst_ref=rcv3.at[dy], send_sem=es.at[dy], recv_sem=er.at[dy],
            device_id=(me, yl * 2 + 1 - core), device_id_type=MESH,
        )

    def project(pair, c):
        ws = []
        for dy in pair:
            y = lax.rem(yl + dy, 4)
            ws.append(wall[pl.ds(4 * y + 2 * c, 2)].reshape(128, 1024))
        rows = jnp.concatenate([lhs[i] for i in range(8)], 1)
        return lax.dot_general(
            rows, jnp.concatenate(ws, 0), (((1,), (1,)), ((), ())), preferred_element_type=F32
        )

    for pair in ((2, 1), (3, 0)):
        acc = project(pair, 1 - core)
        for i, dy in enumerate(pair):
            half[dy] = acc[:, 128 * i : 128 * i + 128].astype(BF16)
            swap(dy).start()
    for pair in ((2, 1), (3, 0)):
        acc = project(pair, core)
        for i, dy in enumerate(pair):
            own[dy] = acc[:, 128 * i : 128 * i + 128]
        for dy in pair:
            swap(dy).wait_recv()
            summ[dy] = (own[dy] + rcv3[dy].astype(F32)).astype(BF16)
            for dx in (2, 1, 3, 0):
                px = lax.rem(x + dx, 4)
                py = lax.rem(yl + dy, 4)
                piece = summ.at[dy, pl.ds(pl.multiple_of(128 * px, 128), 128)]
                if dx == 0 and dy == 0:
                    rcv4[x * 4 + yl] = piece[...]
                else:
                    pltpu.make_async_remote_copy(
                        src_ref=piece, dst_ref=rcv4.at[x * 4 + yl], send_sem=fs, recv_sem=fr,
                        device_id=(zy * 4 + px, py * 2 + core), device_id_type=MESH,
                    ).start()
    all4 = pltpu.make_async_remote_copy(
        src_ref=rcv4.at[pl.ds(0, 15)], dst_ref=rcv4.at[pl.ds(0, 15)], send_sem=fs, recv_sem=fr,
        device_id=(me, ch), device_id_type=MESH,
    )

    for c in range(2):
        all1(c).wait_send()
        all2(c).wait_send()
        for cp in gathers[c]:
            cp.wait_send()
    if WT:
        wy.wait_send()
        for cps in ring_a + ring_b:
            for cp in cps:
                cp.wait_send()
    if POST:
        all_post.wait_send()
    for y in range(4):
        swap(y).wait_send()
    all4.wait_recv()

    t = []
    for px in range(4):
        v = rcv4[4 * px].astype(F32)
        for y in range(1, 4):
            v = v + rcv4[4 * px + y].astype(F32)
        t.append(v)
    row_low = lax.broadcasted_iota(jnp.int32, (128, 128), 1) < 64
    for m in range(4):
        a, b = t[(2 * m) % 4], t[(2 * m + 1) % 4]
        if m < 2:
            o = jnp.where(row_low, a, pltpu.roll(b, 64, 1))
        else:
            o = jnp.where(row_low, pltpu.roll(a, 64, 1), b)
        o = o.astype(BF16)
        out[0, :, 128 * m : 128 * m + 128] = o[0:64]
        out[1, :, 128 * m : 128 * m + 128] = o[64:128]
    all4.wait_send()


def on_device(post_gate, pre_gate, signal, long_filter, out_weight):
    cs, tw, mid, last = tables()
    vm = pltpu.VMEM
    dma = pltpu.SemaphoreType.DMA
    scratch = [
        vm((2, 64, 1024), BF16), vm((2, 64, 1024), BF16), vm((64, 1024), BF16),
        vm((2, 64, 1024), BF16),
        vm((128, 128), BF16), vm((4, 128, 128), F32), vm((3, 128, 256), BF16), vm((64, 256), BF16),
        vm((64, 16, 128), BF16), vm((64, 16, 128), BF16),
        vm((64, 8, 128), BF16), vm((64, 8, 128), BF16),
        vm((1024, 128), F32), vm((512, 128), F32),
        vm((1024, 256), F32),
        vm((1024, 128), BF16), vm((1024, 128), BF16), vm((2048, 128), BF16),
        vm((512, 128), F32),
        vm((2, 64, 8, 128), BF16),
        vm((2, 16, 4, 8, 128), BF16),
        vm((4, 2, 128, 128), BF16), vm((4, 2, 128, 128), BF16),
        vm((8, 512, 128), BF16),
        vm((16, 64, 1024), BF16),
        vm((4, 512, 128), BF16),
        vm((4, 512, 128), BF16),
        vm((4, 512, 128), F32),
        vm((4, 512, 128), BF16),
        vm((16, 128, 128), BF16),
        dma((9,)), dma((2,)), dma((2,)), dma, dma, dma((8,)), dma((8,)), dma((8,)), dma((8,)),
        dma, dma, dma((2,)), dma((2,)), dma((6,)), dma((6,)), dma((4,)), dma((4,)), dma, dma,
    ]
    return pl.pallas_call(
        kernel,
        out_shape=jax.ShapeDtypeStruct((2, 64, 512), BF16),
        in_specs=[pl.BlockSpec(memory_space=pl.ANY)] * 9,
        out_specs=pl.BlockSpec(memory_space=pltpu.VMEM),
        scratch_shapes=scratch,
        compiler_params=pltpu.CompilerParams(
            collective_id=0, has_side_effects=True, vmem_limit_bytes=56 * 1024 * 1024
        ),
        cost_estimate=pl.CostEstimate(flops=2_000_000_000, bytes_accessed=4_000_000, transcendentals=0),
    )(pre_gate, signal, long_filter, post_gate, out_weight.T, cs, tw, mid, last)


def solution(mesh):
    return jax.shard_map(
        on_device,
        mesh=mesh,
        in_specs=(
            P(None, "ctx", "ch"),
            P(None, "ctx", "ch"),
            P(None, "ctx", "ch"),
            P("ctx", "ch"),
            P("ch", "ctx"),
        ),
        out_specs=P(None, "ctx", "ch"),
        check_vma=False,
    )
```

time: 297 us -> 77.1 us (0.26)
  the two profiles are of different devices: /device:TPU:4 before, /device:TPU:8 now
where the time goes in v2:
time: 77.1 us; the launch traced here: 77 us
  Pallas kernels  75.4 us (98%)
  local copies, waits for them, and re-layouts  1.57 us (2%)
    pallas_call x1, Pallas kernels, on_device(): pl.pallas_call(kernel, out_shape=jax.ShapeDtypeStruct((2, 64, 512), BF16)...  75.4 us
    unnamed x1, local copies, waits for them, and re-layouts  1.57 us

profile of v2, /device:TPU:8, one launch (start us, length us, event | category | flops | bytes accessed | tf_op | source)
XLA Modules:
  0.0 77.0 jit_solution(1782169211773293277)
XLA Ops:
  0.0 75.4 %shard_map.91 = bf16[2,64,512]{2,1,0:T(8,128)(2,1)} custom-call(bf16[2,64,1024]{2,1,0:T(8,128)(2,1)} %pre_h.1, bf16[2,64,1024]{2,1,0:T(8,128)(2,1)} %sig_h.1, bf16[64,1024]{1,0:T(8,128)(2,1)} %fil_h.1, bf16[2,64,1024]{2,1,0:T(8,128)(2,1)} %post_h.1, bf16[64,1024]{1,0:T(8,128)(2,1)} %bitcast.1, bf16[128,128]{1,0:T(8,128)(2,1)} %constant.8.clone.cs_h, ...), custom_call_target="tpu_custom_call" | custom-call | flops 2000000000 | bytes 4000000 | tf_op jit(solution)/shard_map/pallas_call | solution.py:445
  75.4 1.6 %copy.11 = bf16[2,64,512]{2,1,0:T(8,128)(2,1)} copy(bf16[2,64,512]{2,1,0:T(8,128)(2,1)} %shard_map.91) | data formatting | bytes 262144

commit v3 on v2

--- a/solution.py
+++ b/solution.py
@@ -10,8 +10,7 @@
 from jax.sharding import PartitionSpec as P
 
 WT, POST = True, True
-PLAN = {"scatter1": ("a1",), "filter0": ("a2",), "back0": ("b1",), "recv1": ("a3",), "back1": ("b2", "a4"), "gather0": ("b3",), "gather1": ("b4", "a5"), "matmul": ("b5",)}
-WY_FIRST = False
+PLAN = {"scatter0": ("w0", "a1"), "filter0": ("a2",), "back0": ("b1",), "recv1": ("a3",), "back1": ("b2",), "gather1": ("a4", "b3"), "kn": ("b4",), "kfd": ("a5", "b5")}
 MESH = pl.DeviceIdType.MESH
 F32 = jnp.float32
 BF16 = jnp.bfloat16
@@ -177,16 +176,15 @@
 
     def at(name):
         for op in PLAN.get(name, ()):
-            step_w(op[0], int(op[1]))
+            if op != "w0":
+                step_w(op[0], int(op[1]))
+            elif WT:
+                wy.start()
 
     loads[3].wait()
-    if WT and WY_FIRST:
-        wy.start()
     scatter(0)
     at("scatter0")
     scatter(1)
-    if WT and not WY_FIRST:
-        wy.start()
     at("scatter1")
 
     loads[4].wait()
@@ -336,45 +334,64 @@
             cp.wait_recv()
     at("matmul")
 
-    def swap(dy):
+    def swap(k):
         return pltpu.make_async_remote_copy(
-            src_ref=half.at[dy], dst_ref=rcv3.at[dy], send_sem=es.at[dy], recv_sem=er.at[dy],
+            src_ref=half.at[k], dst_ref=rcv3.at[k], send_sem=es.at[k], recv_sem=er.at[k],
             device_id=(me, yl * 2 + 1 - core), device_id_type=MESH,
         )
 
-    def project(pair, c):
-        ws = []
-        for dy in pair:
-            y = lax.rem(yl + dy, 4)
-            ws.append(wall[pl.ds(4 * y + 2 * c, 2)].reshape(128, 1024))
+    def target(k):
+        return lax.rem(z // 2 + k, 4)
+
+    def project(k):
+        y = target(k)
+        ws = [wall[pl.ds(4 * y + 2 * c, 2)].reshape(128, 1024) for c in (1 - core, core)]
         rows = jnp.concatenate([lhs[i] for i in range(8)], 1)
-        return lax.dot_general(
+        acc = lax.dot_general(
             rows, jnp.concatenate(ws, 0), (((1,), (1,)), ((), ())), preferred_element_type=F32
         )
-
-    for pair in ((2, 1), (3, 0)):
-        acc = project(pair, 1 - core)
-        for i, dy in enumerate(pair):
-            half[dy] = acc[:, 128 * i : 128 * i + 128].astype(BF16)
-            swap(dy).start()
-    for pair in ((2, 1), (3, 0)):
-        acc = project(pair, core)
-        for i, dy in enumerate(pair):
-            own[dy] = acc[:, 128 * i : 128 * i + 128]
-        for dy in pair:
-            swap(dy).wait_recv()
-            summ[dy] = (own[dy] + rcv3[dy].astype(F32)).astype(BF16)
-            for dx in (2, 1, 3, 0):
-                px = lax.rem(x + dx, 4)
-                py = lax.rem(yl + dy, 4)
-                piece = summ.at[dy, pl.ds(pl.multiple_of(128 * px, 128), 128)]
-                if dx == 0 and dy == 0:
+        half[k] = acc[:, 0:128].astype(BF16)
+        swap(k).start()
+        own[k] = acc[:, 128:256]
+
+    def deliver(k):
+        y = target(k)
+        swap(k).wait_recv()
+        summ[k] = (own[k] + rcv3[k].astype(F32)).astype(BF16)
+        for dx in (2, 1, 3, 0):
+            px = lax.rem(x + dx, 4)
+            piece = summ.at[k, pl.ds(pl.multiple_of(128 * px, 128), 128)]
+
+            def send(piece=piece, px=px):
+                pltpu.make_async_remote_copy(
+                    src_ref=piece, dst_ref=rcv4.at[x * 4 + yl], send_sem=fs, recv_sem=fr,
+                    device_id=(zy * 4 + px, y * 2 + core), device_id_type=MESH,
+                ).start()
+
+            if dx:
+                send()
+            else:
+                pl.when(y != yl)(send)
+
+                @pl.when(y == yl)
+                def _():
                     rcv4[x * 4 + yl] = piece[...]
-                else:
-                    pltpu.make_async_remote_copy(
-                        src_ref=piece, dst_ref=rcv4.at[x * 4 + yl], send_sem=fs, recv_sem=fr,
-                        device_id=(zy * 4 + px, py * 2 + core), device_id_type=MESH,
-                    ).start()
+
+    near = 3 - 2 * lax.rem(z, 2)
+    project(0)
+    at("k0")
+    deliver(0)
+    at("k0d")
+    project(near)
+    at("kn")
+    deliver(near)
+    at("knd")
+    project(4 - near)
+    at("kf")
+    deliver(4 - near)
+    at("kfd")
+    project(2)
+    deliver(2)
     all4 = pltpu.make_async_remote_copy(
         src_ref=rcv4.at[pl.ds(0, 15)], dst_ref=rcv4.at[pl.ds(0, 15)], send_sem=fs, recv_sem=fr,
         device_id=(me, ch), device_id_type=MESH,

time: 77.1 us -> 73.6 us (0.955)
  the two profiles are of different devices: /device:TPU:8 before, /device:TPU:81 now
where the time goes in v3:
time: 73.6 us; the launch traced here: 73.5 us
  Pallas kernels  71.9 us (98%)
  local copies, waits for them, and re-layouts  1.57 us (2%)
    pallas_call x1, Pallas kernels, on_device(): pl.pallas_call(kernel, out_shape=jax.ShapeDtypeStruct((2, 64, 512), BF16)...  71.9 us
    unnamed x1, local copies, waits for them, and re-layouts  1.57 us

profile of v3, /device:TPU:81, one launch (start us, length us, event | category | flops | bytes accessed | tf_op | source)
XLA Modules:
  0.0 73.5 jit_solution(2526698051296179068)
XLA Ops:
  0.0 71.9 %shard_map.91 = bf16[2,64,512]{2,1,0:T(8,128)(2,1)} custom-call(bf16[2,64,1024]{2,1,0:T(8,128)(2,1)} %pre_h.1, bf16[2,64,1024]{2,1,0:T(8,128)(2,1)} %sig_h.1, bf16[64,1024]{1,0:T(8,128)(2,1)} %fil_h.1, bf16[2,64,1024]{2,1,0:T(8,128)(2,1)} %post_h.1, bf16[64,1024]{1,0:T(8,128)(2,1)} %bitcast.1, bf16[128,128]{1,0:T(8,128)(2,1)} %constant.8.clone.cs_h, ...), custom_call_target="tpu_custom_call" | custom-call | flops 2000000000 | bytes 4000000 | tf_op jit(solution)/shard_map/pallas_call | solution.py:462
  71.9 1.6 %copy.11 = bf16[2,64,512]{2,1,0:T(8,128)(2,1)} copy(bf16[2,64,512]{2,1,0:T(8,128)(2,1)} %shard_map.91) | data formatting | bytes 262144

commit v4 on v3

--- a/solution.py
+++ b/solution.py
@@ -379,10 +379,8 @@
 
     near = 3 - 2 * lax.rem(z, 2)
     project(0)
-    at("k0")
+    project(near)
     deliver(0)
-    at("k0d")
-    project(near)
     at("kn")
     deliver(near)
     at("knd")
@@ -442,10 +440,10 @@
         vm((128, 128), BF16), vm((4, 128, 128), F32), vm((3, 128, 256), BF16), vm((64, 256), BF16),
         vm((64, 16, 128), BF16), vm((64, 16, 128), BF16),
         vm((64, 8, 128), BF16), vm((64, 8, 128), BF16),
-        vm((1024, 128), F32), vm((512, 128), F32),
+        vm((1040, 128), F32), vm((520, 128), F32),
         vm((1024, 256), F32),
         vm((1024, 128), BF16), vm((1024, 128), BF16), vm((2048, 128), BF16),
-        vm((512, 128), F32),
+        vm((520, 128), F32),
         vm((2, 64, 8, 128), BF16),
         vm((2, 16, 4, 8, 128), BF16),
         vm((4, 2, 128, 128), BF16), vm((4, 2, 128, 128), BF16),

time: 73.6 us -> 73.6 us (level)
  the two profiles are of different devices: /device:TPU:81 before, /device:TPU:17 now
where the time goes in v4:
time: 73.6 us; the launch traced here: 73.4 us
  Pallas kernels  71.9 us (98%)
  local copies, waits for them, and re-layouts  1.57 us (2%)
    pallas_call x1, Pallas kernels, on_device(): pl.pallas_call(kernel, out_shape=jax.ShapeDtypeStruct((2, 64, 512), BF16)...  71.9 us
    unnamed x1, local copies, waits for them, and re-layouts  1.57 us

profile of v4, /device:TPU:17, one launch (start us, length us, event | category | flops | bytes accessed | tf_op | source)
XLA Modules:
  0.0 73.4 jit_solution(10326556855075895010)
XLA Ops:
  0.0 71.9 %shard_map.91 = bf16[2,64,512]{2,1,0:T(8,128)(2,1)} custom-call(bf16[2,64,1024]{2,1,0:T(8,128)(2,1)} %pre_h.1, bf16[2,64,1024]{2,1,0:T(8,128)(2,1)} %sig_h.1, bf16[64,1024]{1,0:T(8,128)(2,1)} %fil_h.1, bf16[2,64,1024]{2,1,0:T(8,128)(2,1)} %post_h.1, bf16[64,1024]{1,0:T(8,128)(2,1)} %bitcast.1, bf16[128,128]{1,0:T(8,128)(2,1)} %constant.8.clone.cs_h, ...), custom_call_target="tpu_custom_call" | custom-call | flops 2000000000 | bytes 4000000 | tf_op jit(solution)/shard_map/pallas_call | solution.py:460
  71.9 1.6 %copy.11 = bf16[2,64,512]{2,1,0:T(8,128)(2,1)} copy(bf16[2,64,512]{2,1,0:T(8,128)(2,1)} %shard_map.91) | data formatting | bytes 262144
